TPU v7x, 32 devices: a whole 2x2x4 slice. The times are simulated.
32 devices in a mesh: dp: 2 (over core), ctx: 16 (over z, y, x).
Axes of the slice: x: 2, y: 2, z: 4, core: 2. Of those that a mesh axis runs over, the one named last changes fastest.
Arguments:
- tokens: bfloat16 [2, 2048, 1024], P('dp', 'ctx'), may hold values from -6 to 6
- cotangent: bfloat16 [2, 2048, 1024], P('dp', 'ctx'), may hold values from -6 to 6
- block_order: int32 [32], replicated, may hold values from 0 to 31, each once
- doc_lengths: int32 [2, 8], P('dp'), may hold values from 1 to 1024, 2048 in all within a row
- routes: int32 [2, 2048, 1], P('dp', 'ctx'), may hold values from 0 to 15; in each aligned block of 128 rows (0 to 127, 128 to 255, ..., all dimensions but the last counted through in order) at most 16 rows name the same one
- w_qkv: float32 [1024, 3072], P(('dp', 'ctx')), may hold values from -0.1875 to 0.1875
- w_out: float32 [1024, 1024], P(('dp', 'ctx')), may hold values from -3 to 3
- w_up: float32 [1024, 4096], P(('dp', 'ctx')), may hold values from -0.1875 to 0.1875
- w_down: float32 [4096, 1024], P(('dp', 'ctx')), may hold values from -0.09375 to 0.09375
- router: float32 [1024, 18], P(('dp', 'ctx')), may hold values from -0.09375 to 0.09375
- norm_gains: float32 [2, 1024], P(None, ('dp', 'ctx')), may hold values from 0.5 to 1.5
- norm_biases: float32 [2, 1024], P(None, ('dp', 'ctx')), may hold values from -1 to 1
- expert_up: bfloat16 [16, 1024, 4096], P('ctx', None, 'dp'), may hold values from -0.1875 to 0.1875
- expert_down: bfloat16 [16, 4096, 1024], P('ctx', 'dp'), may hold values from -8 to 8
Outputs:
- layer_out: bfloat16 [2, 2048, 1024], P('dp', 'ctx')
- grad_tokens: bfloat16 [2, 2048, 1024], P('dp', 'ctx')
- grad_w_qkv: float32 [1024, 3072], P(('dp', 'ctx'))
- grad_w_out: float32 [1024, 1024], P(('dp', 'ctx'))
- grad_w_up: float32 [1024, 4096], P(('dp', 'ctx'))
- grad_w_down: float32 [4096, 1024], P(('dp', 'ctx'))
- grad_router: float32 [1024, 18], P(('dp', 'ctx'))
- grad_norm_gains: float32 [2, 1024], P(None, ('dp', 'ctx'))
- grad_norm_biases: float32 [2, 1024], P(None, ('dp', 'ctx'))
- grad_expert_up: float32 [16, 1024, 4096], P('ctx', None, 'dp')
- grad_expert_down: float32 [16, 4096, 1024], P('ctx', 'dp')
Inputs may be any that keep to these rules, and one draw needn't show every extreme that they name: `block_order`: each value appears once; entry i is the initial block place, in blocks of 64 tokens, of rows i * 64 to (i + 1) * 64 - 1 of every packed sequence. `doc_lengths`: A packed sequence's document lengths sum to 2048; the longest is exactly 1024. `routes`: among the 128 rows of a packed sequence that one index of ctx holds, no expert is named more than 16 times, a bound that some block reaches.
All inputs are finite; a program needn't handle non-finite values.
Results may differ from a plain program's by a relative error of at most 0.014.
Values may be sent and summed in bfloat16 or wider, within the bound.
A program may use at most 320 MiB of HBM per device.

v0:
```python
import math

import jax
import jax.numpy as jnp
from jax import lax
from jax.sharding import PartitionSpec as P

HEADS = 16
HEAD_DIM = 64


EPS = 1e-05
NEG = -1e30
SCALE = 0.125


def layer_norm(values, gain, shift):
    center = values - jnp.mean(values, axis=-1, keepdims=True)
    spread = jnp.mean(center * center, axis=-1, keepdims=True)
    return center * lax.rsqrt(spread + EPS) * gain + shift


def gelu_tanh(values):
    return jax.nn.gelu(values, approximate=True)


def router_heads(router_logits, route_hot, experts):
    chances = jax.nn.softmax(router_logits[:, :experts], axis=-1)
    gate = jnp.sum(chances * route_hot, axis=-1)
    mixing = jax.nn.softmax(router_logits[:, experts:], axis=-1)
    return (gate, mixing[:, 0], mixing[:, 1])


def place_rows(rows, block_order, block_rows, doc_ends):
    blocks = rows // block_rows
    marks = blocks[:, None] == jnp.arange(block_order.shape[0], dtype=jnp.int32)[None, :]
    anchor = jnp.sum(jnp.where(marks, block_order[None, :], 0), axis=1)
    place = anchor * block_rows + rows % block_rows
    document = jnp.sum((doc_ends[None, :] <= place[:, None]).astype(jnp.int32), axis=1)
    return (place, document)


def score_block(query_part, key_part, query_place, query_doc, key_place, key_doc):
    raw = jnp.einsum("qhd,khd->hqk", query_part, key_part, preferred_element_type=jnp.float32)
    allowed = (key_place[None, :] <= query_place[:, None]) & (
        key_doc[None, :] == query_doc[:, None]
    )
    return (raw * SCALE, allowed[None])


def contract_rows(left, right):
    return lax.dot_general(
        left, right, (((0,), (0,)), ((), ())), preferred_element_type=jnp.float32
    )


def contract_cols(left, right):
    return lax.dot_general(
        left, right, (((1,), (1,)), ((), ())), preferred_element_type=jnp.float32
    )


def unpack(params):
    qkv_weight, out_weight, up_weight, down_weight, router_weight, gains_low, biases_low = params
    return (
        qkv_weight,
        out_weight,
        up_weight,
        down_weight,
        router_weight,
        gains_low.astype(jnp.float32),
        biases_low.astype(jnp.float32),
    )


def per_device(
    tokens,
    cotangent,
    block_order,
    doc_lengths,
    routes,
    w_qkv,
    w_out,
    w_up,
    w_down,
    router,
    norm_gains,
    norm_biases,
    expert_up,
    expert_down,
):
    rows = tokens.shape[1]
    width = tokens.shape[2]
    ctx_count = lax.axis_size("ctx")
    length = rows * ctx_count
    experts = ctx_count * expert_up.shape[0]
    capacity = max(2, 2 * rows // experts)
    block_rows = length // block_order.shape[0]
    doc_ends = jnp.cumsum(doc_lengths[0])
    own_rows = lax.axis_index("ctx") * rows + jnp.arange(rows, dtype=jnp.int32)
    own_place, own_doc = place_rows(own_rows, block_order, block_rows, doc_ends)
    all_place, all_doc = place_rows(
        jnp.arange(length, dtype=jnp.int32), block_order, block_rows, doc_ends
    )
    masters = (
        w_qkv.astype(jnp.bfloat16),
        w_out.astype(jnp.bfloat16),
        w_up.astype(jnp.bfloat16),
        w_down.astype(jnp.bfloat16),
        router.astype(jnp.bfloat16),
        norm_gains.astype(jnp.bfloat16),
        norm_biases.astype(jnp.bfloat16),
    )
    params = (
        lax.all_gather(masters[0], ("dp", "ctx"), axis=0, tiled=True),
        lax.all_gather(masters[1], ("dp", "ctx"), axis=0, tiled=True),
        lax.all_gather(masters[2], ("dp", "ctx"), axis=0, tiled=True),
        lax.all_gather(masters[3], ("dp", "ctx"), axis=0, tiled=True),
        lax.all_gather(masters[4], ("dp", "ctx"), axis=0, tiled=True),
        lax.all_gather(masters[5], ("dp", "ctx"), axis=1, tiled=True),
        lax.all_gather(masters[6], ("dp", "ctx"), axis=1, tiled=True),
    )
    qkv_weight, out_weight, up_weight, down_weight, router_weight, gains, shifts = unpack(params)
    inputs = tokens[0].astype(jnp.float32)
    normed_low = layer_norm(inputs, gains[0], shifts[0]).astype(jnp.bfloat16)
    mixed_low = jnp.dot(normed_low, qkv_weight, preferred_element_type=jnp.float32).astype(
        jnp.bfloat16
    )
    queries = mixed_low[:, :width].reshape(rows, HEADS, HEAD_DIM)
    gathered = lax.all_gather(mixed_low[:, width:], "ctx", axis=0, tiled=True)
    key_block = math.gcd(length, 1024)
    key_count = length // key_block
    key_stack = gathered[:, :width].reshape(key_count, key_block, HEADS, HEAD_DIM)
    value_stack = gathered[:, width:].reshape(key_count, key_block, HEADS, HEAD_DIM)
    stacks = (
        key_stack,
        value_stack,
        all_place.reshape(key_count, key_block),
        all_doc.reshape(key_count, key_block),
    )

    def peak_step(carry, block):
        peak, total = carry
        key_part, value_part, key_place, key_doc = block
        scores, allowed = score_block(queries, key_part, own_place, own_doc, key_place, key_doc)
        masked = jnp.where(allowed, scores, NEG)
        new_peak = jnp.maximum(peak, jnp.max(masked, axis=2))
        weights = jnp.where(allowed, jnp.exp(masked - new_peak[:, :, None]), 0.0)
        total = total * jnp.exp(peak - new_peak) + jnp.sum(weights, axis=2)
        return ((new_peak, total), None)

    start_peak = jnp.full((HEADS, rows), NEG, jnp.float32)
    (peak, total), nothing = lax.scan(
        peak_step, (start_peak, jnp.zeros((HEADS, rows), jnp.float32)), stacks
    )
    log_total = peak + jnp.log(total)

    def value_step(carry, block):
        key_part, value_part, key_place, key_doc = block
        scores, allowed = score_block(queries, key_part, own_place, own_doc, key_place, key_doc)
        chances = jnp.where(allowed, jnp.exp(scores - log_total[:, :, None]), 0.0)
        added = jnp.einsum(
            "hqk,khd->qhd",
            chances.astype(jnp.bfloat16),
            value_part,
            preferred_element_type=jnp.float32,
        )
        return (carry + added, None)

    attention, nothing = lax.scan(
        value_step, jnp.zeros((rows, HEADS, HEAD_DIM), jnp.float32), stacks
    )
    attended_low = attention.reshape(rows, width).astype(jnp.bfloat16)
    middle = inputs + jnp.dot(attended_low, out_weight, preferred_element_type=jnp.float32)
    second_low = layer_norm(middle, gains[1], shifts[1]).astype(jnp.bfloat16)
    upper_residual = jnp.dot(second_low, up_weight, preferred_element_type=jnp.float32)
    active_low = gelu_tanh(upper_residual).astype(jnp.bfloat16)
    dense_output = jnp.dot(active_low, down_weight, preferred_element_type=jnp.float32)
    router_logits = jnp.dot(second_low, router_weight, preferred_element_type=jnp.float32)
    route = routes[0, :, 0]
    route_hot = (route[:, None] == jnp.arange(experts, dtype=jnp.int32)[None, :]).astype(
        jnp.float32
    )
    gate, mix_dense, mix_expert = router_heads(router_logits, route_hot, experts)
    chosen = route_hot.astype(jnp.int32)
    ranks = jnp.cumsum(chosen, axis=0) - 1
    slot = jnp.sum(jnp.where(chosen > 0, ranks, 0), axis=1)
    target = route * capacity + slot
    select = (jnp.arange(experts * capacity, dtype=jnp.int32)[:, None] == target[None, :]).astype(
        jnp.bfloat16
    )
    send = jnp.dot(select, second_low, preferred_element_type=jnp.float32).astype(jnp.bfloat16)
    arrived = lax.all_to_all(
        jnp.concatenate([send, send], axis=0),
        ("dp", "ctx"),
        split_axis=0,
        concat_axis=0,
        tiled=True,
    )
    expert_hidden = jnp.dot(arrived, expert_up[0], preferred_element_type=jnp.float32)
    expert_active = gelu_tanh(expert_hidden).astype(jnp.bfloat16)
    partial_out = jnp.dot(expert_active, expert_down[0], preferred_element_type=jnp.float32)
    returned = lax.all_to_all(partial_out, ("dp", "ctx"), split_axis=0, concat_axis=0, tiled=True)
    half = experts * capacity
    expert_rows = jnp.take(returned[:half] + returned[half:], target, axis=0)
    scaled_gate = mix_expert * gate
    layer_out = middle + mix_dense[:, None] * dense_output + scaled_gate[:, None] * expert_rows
    out_grad = cotangent[0].astype(jnp.float32)
    dense_grad = (out_grad * mix_dense[:, None]).astype(jnp.bfloat16)
    active_grad = contract_cols(dense_grad, down_weight)
    upper_pull = jax.vjp(gelu_tanh, upper_residual)[1]
    upper_grad = upper_pull(active_grad)[0].astype(jnp.bfloat16)
    down_term = contract_rows(active_low, dense_grad)
    up_term = contract_rows(second_low, upper_grad)
    second_grad = contract_cols(upper_grad, up_weight)
    expert_dot = jnp.sum(out_grad * expert_rows, axis=1)
    dense_dot = jnp.sum(out_grad * dense_output, axis=1)
    router_pull = jax.vjp(lambda values: router_heads(values, route_hot, experts), router_logits)[1]
    logit_grad = router_pull((expert_dot * mix_expert, dense_dot, expert_dot * gate))[0].astype(
        jnp.bfloat16
    )
    router_term = contract_rows(second_low, logit_grad)
    second_grad = second_grad + contract_cols(logit_grad, router_weight)
    expert_grad = (out_grad * scaled_gate[:, None]).astype(jnp.bfloat16)
    grad_send = jnp.dot(select, expert_grad, preferred_element_type=jnp.float32).astype(
        jnp.bfloat16
    )
    arrived_grad = lax.all_to_all(
        jnp.concatenate([grad_send, grad_send], axis=0),
        ("dp", "ctx"),
        split_axis=0,
        concat_axis=0,
        tiled=True,
    )
    expert_down_grad = contract_rows(expert_active, arrived_grad)
    hidden_pull = jax.vjp(gelu_tanh, expert_hidden)[1]
    hidden_grad = hidden_pull(contract_cols(arrived_grad, expert_down[0]))[0].astype(jnp.bfloat16)
    expert_up_grad = contract_rows(arrived, hidden_grad)
    input_part = contract_cols(hidden_grad, expert_up[0])
    returned_grad = lax.all_to_all(
        input_part, ("dp", "ctx"), split_axis=0, concat_axis=0, tiled=True
    )
    second_grad = second_grad + jnp.take(
        returned_grad[:half] + returned_grad[half:], target, axis=0
    )
    second_pull = jax.vjp(layer_norm, middle, gains[1], shifts[1])[1]
    middle_part, gain_second, bias_second = second_pull(second_grad)
    middle_grad = out_grad + middle_part
    branch_grad = middle_grad.astype(jnp.bfloat16)
    out_term = contract_rows(attended_low, branch_grad)
    attended_grad = (
        contract_cols(branch_grad, out_weight).astype(jnp.bfloat16).reshape(rows, HEADS, HEAD_DIM)
    )
    delta = jnp.einsum("qhd,qhd->hq", attended_grad.astype(jnp.float32), attention)
    zero_rows = jnp.zeros((rows, HEADS, HEAD_DIM), jnp.float32)

    def key_grad_step(carry, block):
        key_part, value_part, key_place, key_doc = block
        scores, allowed = score_block(queries, key_part, own_place, own_doc, key_place, key_doc)
        chances = jnp.where(allowed, jnp.exp(scores - log_total[:, :, None]), 0.0)
        flow = jnp.einsum(
            "qhd,khd->hqk", attended_grad, value_part, preferred_element_type=jnp.float32
        )
        score_grad = (chances * (flow - delta[:, :, None]) * SCALE).astype(jnp.bfloat16)
        carry = carry + jnp.einsum(
            "hqk,khd->qhd", score_grad, key_part, preferred_element_type=jnp.float32
        )
        key_term = jnp.einsum(
            "hqk,qhd->khd", score_grad, queries, preferred_element_type=jnp.float32
        ).reshape(key_block, width)
        value_term = jnp.einsum(
            "hqk,qhd->khd",
            chances.astype(jnp.bfloat16),
            attended_grad,
            preferred_element_type=jnp.float32,
        ).reshape(key_block, width)
        return (carry, jnp.concatenate([key_term, value_term], axis=1))

    query_total, pair_terms = lax.scan(key_grad_step, zero_rows, stacks)
    pair_grad = lax.psum_scatter(
        pair_terms.reshape(length, 2 * width), "ctx", scatter_dimension=0, tiled=True
    )
    query_grad = query_total.reshape(rows, width)
    key_grad = pair_grad[:, :width]
    value_grad = pair_grad[:, width:]
    mixed_grad = jnp.concatenate([query_grad, key_grad, value_grad], axis=1).astype(jnp.bfloat16)
    qkv_term = contract_rows(normed_low, mixed_grad)
    normed_grad = contract_cols(mixed_grad, qkv_weight)
    first_pull = jax.vjp(layer_norm, inputs, gains[0], shifts[0])[1]
    input_part_grad, gain_first, bias_first = first_pull(normed_grad)
    input_grad = middle_grad + input_part_grad
    gain_terms = jnp.stack([gain_first, gain_second])
    bias_terms = jnp.stack([bias_first, bias_second])
    sums = (
        lax.psum_scatter(qkv_term, ("dp", "ctx"), scatter_dimension=0, tiled=True),
        lax.psum_scatter(out_term, ("dp", "ctx"), scatter_dimension=0, tiled=True),
        lax.psum_scatter(up_term, ("dp", "ctx"), scatter_dimension=0, tiled=True),
        lax.psum_scatter(down_term, ("dp", "ctx"), scatter_dimension=0, tiled=True),
        lax.psum_scatter(router_term, ("dp", "ctx"), scatter_dimension=0, tiled=True),
        lax.psum_scatter(gain_terms, ("dp", "ctx"), scatter_dimension=1, tiled=True),
        lax.psum_scatter(bias_terms, ("dp", "ctx"), scatter_dimension=1, tiled=True),
    )
    return (
        layer_out[None].astype(jnp.bfloat16),
        input_grad[None].astype(jnp.bfloat16),
        sums[0],
        sums[1],
        sums[2],
        sums[3],
        sums[4],
        sums[5],
        sums[6],
        expert_up_grad[None],
        expert_down_grad[None],
    )


def solution(mesh):
    in_specs = (
        P("dp", "ctx", None),
        P("dp", "ctx", None),
        P(),
        P("dp", None),
        P("dp", "ctx", None),
        P(("dp", "ctx"), None),
        P(("dp", "ctx"), None),
        P(("dp", "ctx"), None),
        P(("dp", "ctx"), None),
        P(("dp", "ctx"), None),
        P(None, ("dp", "ctx")),
        P(None, ("dp", "ctx")),
        P("ctx", None, "dp"),
        P("ctx", "dp", None),
    )
    out_specs = (
        P("dp", "ctx", None),
        P("dp", "ctx", None),
        P(("dp", "ctx"), None),
        P(("dp", "ctx"), None),
        P(("dp", "ctx"), None),
        P(("dp", "ctx"), None),
        P(("dp", "ctx"), None),
        P(None, ("dp", "ctx")),
        P(None, ("dp", "ctx")),
        P("ctx", None, "dp"),
        P("ctx", "dp", None),
    )
    return jax.shard_map(
        per_device, mesh=mesh, in_specs=in_specs, out_specs=out_specs, check_vma=False
    )
```

profile of v0, /device:TPU:0, one launch (start us, length us, event | category | flops | bytes accessed | tf_op | source)
XLA Modules:
  0.0 2527.5 jit_solution(17319687350338213174)
XLA Ops:
  9.7 69.5 %all-gather.1 = bf16[32,32,2]{1,2,0:T(2,128)(2,1)S(1)} all-gather(bf16[1,32,2]{1,2,0:T(2,128)(2,1)S(1)} %convert_bitcast_fusion.2), channel_id=1, replica_groups=mesh['dp'=2,'ctx'=16] {'dp','ctx'}, dimensions={0}, use_global_device_ids=true | all-gather | bytes 4224 | tf_op jit(solution)/shard_map/all_gather | solution.py:121
  79.9 63.0 %all-gather = bf16[32,32,2]{1,2,0:T(2,128)(2,1)S(1)} all-gather(bf16[1,32,2]{1,2,0:T(2,128)(2,1)S(1)} %convert_bitcast_fusion.3), channel_id=1, replica_groups=mesh['dp'=2,'ctx'=16] {'dp','ctx'}, dimensions={0}, use_global_device_ids=true | all-gather | bytes 4224 | tf_op jit(solution)/shard_map/all_gather | solution.py:120
  154.4 108.0 %all-gather.11.cloned.1.call-done = bf16[2048,2048]{1,0:T(8,128)(2,1)} async-done(((bf16[128,2048]{1,0:T(8,128)(2,1)}), bf16[2048,2048]{1,0:T(8,128)(2,1)}) %all-gather.11.cloned.1.call-update) | async-done | bytes 8388624 | tf_op jit(solution)/shard_map/all_gather | solution.py:130
  268.5 11.5 reshape.515
  280.1 9.8 copy.128
  289.8 11.5 reshape.516
  301.4 9.8 copy.129
  311.2 23.5 while.37
  334.8 10.8 while.38
  348.9 42.2 %all_to_all.36 = bf16[32,16,1024]{2,1,0:T(8,128)(2,1)S(1)} all-to-all(bf16[32,16,1024]{2,1,0:T(8,128)(2,1)S(1)} %bitcast.333), channel_id=1, replica_groups=mesh['dp'=2,'ctx'=16] {'dp','ctx'}, dimensions={0} | all-to-all | bytes 2097152 | tf_op jit(solution)/shard_map/all_to_all | solution.py:193
  404.9 119.3 %all-gather.2 = bf16[32,32,18]{1,2,0:T(8,128)(2,1)S(1)} all-gather(bf16[1,32,18]{1,2,0:T(8,128)(2,1)S(1)} %convert_bitcast_fusion.1), channel_id=1, replica_groups=mesh['dp'=2,'ctx'=16] {'dp','ctx'}, dimensions={0}, use_global_device_ids=true | all-gather | bytes 38016 | tf_op jit(solution)/shard_map/all_gather | solution.py:119
  540.4 30.9 %all_to_all.37 = bf16[32,16,1024]{2,1,0:T(8,128)(2,1)S(1)} all-to-all(bf16[32,16,1024]{2,1,0:T(8,128)(2,1)S(1)} %bitcast.334), channel_id=1, replica_groups=mesh['dp'=2,'ctx'=16] {'dp','ctx'}, dimensions={0} | all-to-all | bytes 2097152 | tf_op jit(solution)/shard_map/all_to_all | solution.py:228
  599.8 35.4 %all-to-all-done.3 = f32[32,16,1024]{2,1,0:T(8,128)} async-done(((f32[32,16,1024]{2,1,0:T(8,128)}), f32[32,16,1024]{2,1,0:T(8,128)}, u32[]{:S(2)}, u32[]{:S(2)}) %all-to-all-start.3) | async-done | bytes 2097184 | tf_op jit(solution)/shard_map/all_to_all | solution.py:240
  644.9 80.5 %while.39 = (s32[]{:T(128)}, f32[128,16,64]{0,2,1:T(8,128)S(1)}, f32[2,1024,2048]{2,1,0:T(8,128)}, bf16[2,1024,16,64]{1,3,2,0:T(8,128)(2,1)}, s32[2,1024]{1,0:T(...) while((s32[]{:T(128)}, f32[128,16,64]{0,2,1:T(8,128)S(1)}, ...), condition=%wide.region_29.31_spmd.clone, body=%wide.region_28.30_spmd.clone.sunk | while | flops 1367998464 | bytes 172410128 | solution.py:279
  668.4 9.1 copy.189
  708.5 9.1 copy.189
  727.7 340.9 %reduce-scatter.15.cloned.1.call-done = f32[128,2048]{1,0:T(8,128)} async-done(((f32[2048,2048]{1,0:T(8,128)}), f32[128,2048]{1,0:T(8,128)}) %reduce-scatter.15.cloned.1.call-update) | async-done | bytes 1048592 | tf_op jit(solution)/shard_map/reduce_scatter | solution.py:280
  1105.7 108.6 %reduce-scatter.25.cloned.1.call-done = f32[32,18]{1,0:T(8,128)} async-done(((f32[1024,18]{1,0:T(8,128)}), f32[32,18]{1,0:T(8,128)}) %reduce-scatter.25.cloned.1.call-update) | async-done | bytes 2320
  1230.1 120.5 %reduce-scatter.27.cloned.1.call-done = f32[32,2]{1,0:T(8,128)} async-done(((f32[1024,2]{1,0:T(8,128)}), f32[32,2]{1,0:T(8,128)}) %reduce-scatter.27.cloned.1.call-update) | async-done | bytes 272
  1351.9 134.9 %reduce-scatter.29.cloned.1.call-done = f32[32,2]{1,0:T(8,128)} async-done(((f32[1024,2]{1,0:T(8,128)}), f32[32,2]{1,0:T(8,128)}) %reduce-scatter.29.cloned.1.call-update) | async-done | bytes 272
  1488.2 145.7 %reduce-scatter.19.cloned.1.call-done = f32[32,1024]{1,0:T(8,128)} async-done(((f32[1024,1024]{1,0:T(8,128)}), f32[32,1024]{1,0:T(8,128)}) %reduce-scatter.19.cloned.1.call-update) | async-done | bytes 131088 | tf_op jit(solution)/shard_map/reduce_scatter | solution.py:296
  1633.9 358.1 %reduce-scatter.21.cloned.1.call-done = f32[32,4096]{1,0:T(8,128)} async-done(((f32[1024,4096]{1,0:T(8,128)}), f32[32,4096]{1,0:T(8,128)}) %reduce-scatter.21.cloned.1.call-update) | async-done | bytes 524304 | tf_op jit(solution)/shard_map/reduce_scatter | solution.py:297
  1992.0 362.8 %reduce-scatter.23.cloned.1.call-done = f32[128,1024]{1,0:T(8,128)} async-done(((f32[4096,1024]{1,0:T(8,128)}), f32[128,1024]{1,0:T(8,128)}) %reduce-scatter.23.cloned.1.call-update) | async-done | bytes 524304 | tf_op jit(solution)/shard_map/reduce_scatter | solution.py:298
  2354.9 165.7 %reduce-scatter.17.cloned.1.call-done = f32[32,3072]{1,0:T(8,128)} async-done(((f32[1024,3072]{1,0:T(8,128)}), f32[32,3072]{1,0:T(8,128)}) %reduce-scatter.17.cloned.1.call-update) | async-done | bytes 393232 | tf_op jit(solution)/shard_map/reduce_scatter | solution.py:295
  (318 shorter events, 245.1 us)
Async XLA Ops:
  7.2 138.2 %all-gather.9.cloned.1.call-start = ((), (), s32[]{:S(2)}) async-start(), calls=%async_computation.12 | async-start | bytes 6488064 | tf_op jit(solution)/shard_map/all_gather | solution.py:115
  8.9 253.5 %all-gather.11.cloned.1.call-start = ((), (), s32[]{:S(2)}) async-start(), calls=%async_computation.13 | async-start | bytes 8912896 | tf_op jit(solution)/shard_map/all_gather | solution.py:130
  150.7 195.0 %all-gather.13.cloned.1.call-start = ((), (), s32[]{:S(2)}) async-start(), calls=%async_computation.14 | async-start | bytes 2162688 | tf_op jit(solution)/shard_map/all_gather | solution.py:116
  151.5 373.3 %all-gather.15.cloned.1.call-start = ((), (), s32[]{:S(2)}) async-start(), calls=%async_computation.15 | async-start | bytes 8650752 | tf_op jit(solution)/shard_map/all_gather | solution.py:117
  152.3 381.0 %all-gather.17.cloned.1.call-start = ((), (), s32[]{:S(2)}) async-start(), calls=%async_computation.16 | async-start | bytes 8650752 | tf_op jit(solution)/shard_map/all_gather | solution.py:118
  345.7 45.4 %copy-start.55 = (bf16[1,1024,2048]{2,1,0:T(8,128)(2,1)S(1)}, bf16[1,1024,2048]{2,1,0:T(8,128)(2,1)}, u32[]{:S(2)}) copy-start(bf16[1,1024,2048]{2,1,0:T(8,128)(2,1)} %param.34) | copy-start | bytes 12582916
  348.5 176.3 %copy-start.4 = (bf16[128,1024]{1,0:T(8,128)(2,1)}, bf16[128,1024]{1,0:T(8,128)(2,1)S(1)}, u32[]{:S(2)}) copy-start(bf16[128,1024]{1,0:T(8,128)(2,1)S(1)} %add_convert_fusion.2) | copy-start | bytes 786436
  401.2 129.5 %all-to-all-start.1 = ((f32[32,16,1024]{2,1,0:T(8,128)}), f32[32,16,1024]{2,1,0:T(8,128)}, u32[]{:S(2)}, u32[]{:S(2)}) async-start(f32[32,16,1024]{2,1,0:T(8,128)} %fusion.73), calls=%async_computation.1 | async-start | bytes 4194304 | tf_op jit(solution)/shard_map/all_to_all | solution.py:203
  539.9 101.1 %copy-start.46 = (f32[128]{0:T(128)}, f32[128]{0:T(128)S(1)}, u32[]{:S(2)}) copy-start(f32[128]{0:T(128)S(1)} %get-tuple-element.578) | copy-start | bytes 1540
  581.2 54.1 %all-to-all-start.3 = ((f32[32,16,1024]{2,1,0:T(8,128)}), f32[32,16,1024]{2,1,0:T(8,128)}, u32[]{:S(2)}, u32[]{:S(2)}) async-start(f32[32,16,1024]{2,1,0:T(8,128)} %fusion.71), calls=%async_computation.3 | async-start | bytes 4194304 | tf_op jit(solution)/shard_map/all_to_all | solution.py:240
  584.7 483.9 %reduce-scatter.15.cloned.1.call-start = ((), (), s32[]{:S(2)}) async-start(), calls=%async_computation.17 | async-start | bytes 17825792 | tf_op jit(solution)/shard_map/reduce_scatter | solution.py:280
  584.8 53.7 %copy-start.44 = (f32[128,2]{0,1:T(2,128)}, f32[128,2]{0,1:T(2,128)S(1)}, u32[]{:S(2)}) copy-start(f32[128,2]{0,1:T(2,128)S(1)} %add_multiply_fusion) | copy-start | bytes 3076
  584.8 53.7 %copy-start.34 = (f32[128,16]{0,1:T(8,128)}, f32[128,16]{0,1:T(8,128)S(1)}, u32[]{:S(2)}) copy-start(f32[128,16]{0,1:T(8,128)S(1)} %fusion.130) | copy-start | bytes 24580
  725.4 344.5 %copy-start.3 = (bf16[1,128,1024]{2,1,0:T(8,128)(2,1)S(1)}, bf16[1,128,1024]{2,1,0:T(8,128)(2,1)}, u32[]{:S(2)}) copy-start(bf16[1,128,1024]{2,1,0:T(8,128)(2,1)} %param.22) | copy-start | bytes 786436
  725.4 344.5 %copy-start.30 = (f32[1,1024]{1,0:T(1,128)S(1)}, f32[1,1024]{1,0:T(1,128)}, u32[]{:S(2)}) copy-start(f32[1,1024]{1,0:T(1,128)} %copy-done.29) | copy-start | bytes 12292
  725.5 344.5 %copy-start.37 = (f32[128]{0:T(128)S(1)}, f32[128]{0:T(128)}, u32[]{:S(2)}) copy-start(f32[128]{0:T(128)} %copy-done.36) | copy-start | bytes 1540
  725.5 488.9 %reduce-scatter.25.cloned.1.call-start = ((), (), s32[]{:S(2)}) async-start(), calls=%async_computation.22 | async-start | bytes 540672
  727.4 623.2 %reduce-scatter.27.cloned.1.call-start = ((), (), s32[]{:S(2)}) async-start(), calls=%async_computation.23 | async-start | bytes 540672
  1076.6 410.2 %reduce-scatter.29.cloned.1.call-start = ((), (), s32[]{:S(2)}) async-start(), calls=%async_computation.24 | async-start | bytes 540672
  1077.8 556.1 %reduce-scatter.19.cloned.1.call-start = ((), (), s32[]{:S(2)}) async-start(), calls=%async_computation.19 | async-start | bytes 4325376 | tf_op jit(solution)/shard_map/reduce_scatter | solution.py:296
  1080.7 911.3 %reduce-scatter.21.cloned.1.call-start = ((), (), s32[]{:S(2)}) async-start(), calls=%async_computation.20 | async-start | bytes 17301504 | tf_op jit(solution)/shard_map/reduce_scatter | solution.py:297
  1088.9 1266.0 %reduce-scatter.23.cloned.1.call-start = ((), (), s32[]{:S(2)}) async-start(), calls=%async_computation.21 | async-start | bytes 17301504 | tf_op jit(solution)/shard_map/reduce_scatter | solution.py:298
  1098.6 1421.9 %reduce-scatter.17.cloned.1.call-start = ((), (), s32[]{:S(2)}) async-start(), calls=%async_computation.18 | async-start | bytes 12976128 | tf_op jit(solution)/shard_map/reduce_scatter | solution.py:295
  1105.7 110.1 %copy-start.24 = (bf16[32,16,1024]{2,1,0:T(8,128)(2,1)S(1)}, bf16[32,16,1024]{2,1,0:T(8,128)(2,1)}, u32[]{:S(2)}) copy-start(bf16[32,16,1024]{2,1,0:T(8,128)(2,1)} %copy-done.23) | copy-start | bytes 3145732
  (56 other events, 312.5 us)
Sparse Core Ops, SparseCore 0:
  11.5 72.3 all-gather.8
  150.8 111.5 all-gather.10
  265.9 54.6 all-gather.12
  323.9 91.9 all-gather.14
  419.2 90.1 all-gather.16
  725.6 342.9 reduce-scatter.14
  1071.4 142.8 reduce-scatter.24
  1216.7 133.8 reduce-scatter.26
  1352.8 133.9 reduce-scatter.28
  1489.6 144.2 reduce-scatter.18
  1636.9 355.1 reduce-scatter.20
  1994.9 359.9 reduce-scatter.22
  2362.5 158.0 reduce-scatter.16
where the time goes:
time: 2540 us; the launch traced here: 2530 us
  waiting for transfers between devices  1880 us (74%)
  blocking collectives  325 us (13%)
  matrix products  161 us (6%)
  local copies, waits for them, and re-layouts  99.9 us (4%)
  other arithmetic  37.3 us (1%)
    unnamed x16, waiting for transfers between devices  364 us
    reduce_scatter x1, waiting for transfers between devices, per_device(): lax.psum_scatter(down_term, ('dp', 'ctx'), scatter_dimension=0, tiled=True)  363 us
    reduce_scatter x1, waiting for transfers between devices, per_device(): lax.psum_scatter(up_term, ('dp', 'ctx'), scatter_dimension=0, tiled=True)  358 us
    reduce_scatter x1, waiting for transfers between devices, per_device(): lax.psum_scatter(pair_terms.reshape(length, 2 * width), 'ctx', scatter_di...  341 us
    reduce_scatter x1, waiting for transfers between devices, per_device(): lax.psum_scatter(qkv_term, ('dp', 'ctx'), scatter_dimension=0, tiled=True)  166 us
    reduce_scatter x1, waiting for transfers between devices, per_device(): lax.psum_scatter(out_term, ('dp', 'ctx'), scatter_dimension=0, tiled=True)  146 us
    all_gather x1, blocking collectives, per_device(): lax.all_gather(masters[4], ('dp', 'ctx'), axis=0, tiled=True)  119 us
    all_gather x1, waiting for transfers between devices, per_device(): gathered = lax.all_gather(mixed_low[:, width:], 'ctx', axis=0, tiled=True)  108 us
  transfers between devices with their start and end apart: 15, of which 10 were waited for; matrix products, arithmetic and copies ran while one was open for 7% of the time, Pallas kernels for 0%

commit v1 on v0

v1 whole, which is shorter than its diff:
```python
import functools
import math

import jax
import jax.numpy as jnp
from jax import lax
from jax.experimental import pallas as pl
from jax.experimental.pallas import tpu as pltpu
from jax.sharding import PartitionSpec as P

HEADS = 16
HEAD_DIM = 64

EPS = 1e-05
NEG = -1e30
SCALE = 0.125
TILE = 256
BF = jnp.bfloat16
F32 = jnp.float32
MESH = pl.DeviceIdType.MESH


def layer_norm(values, gain, shift):
    center = values - jnp.mean(values, axis=-1, keepdims=True)
    spread = jnp.mean(center * center, axis=-1, keepdims=True)
    return center * lax.rsqrt(spread + EPS) * gain + shift


def gelu_tanh(values):
    return jax.nn.gelu(values, approximate=True)


def router_heads(router_logits, route_hot, experts):
    chances = jax.nn.softmax(router_logits[:, :experts], axis=-1)
    gate = jnp.sum(chances * route_hot, axis=-1)
    mixing = jax.nn.softmax(router_logits[:, experts:], axis=-1)
    return (gate, mixing[:, 0], mixing[:, 1])


def dot_f32(left, right):
    return jnp.dot(left, right, preferred_element_type=F32)


def contract_rows(left, right):
    return lax.dot_general(left, right, (((0,), (0,)), ((), ())), preferred_element_type=F32)


def contract_cols(left, right):
    return lax.dot_general(left, right, (((1,), (1,)), ((), ())), preferred_element_type=F32)


class Move:
    def __init__(self, step, src, dst, after=None):
        self.step, self.src, self.dst, self.after = step, src, dst, after


def exchange(name, cid, sizes, ins, outs, build):
    two, groups, team = sizes

    def kernel(*refs):
        in_refs, out_refs = refs[: len(ins)], refs[len(ins) : len(ins) + len(outs)]
        send_sem, recv_sem, local_sem = refs[len(ins) + len(outs) :]
        c = lax.axis_index("dp")
        i = lax.axis_index("ctx")
        g, t = lax.div(i, team), lax.rem(i, team)

        def device(step):
            dc, dg, dt = step
            return (
                lax.rem(c + dc, two),
                lax.rem(g + dg, groups) * team + lax.rem(t + dt, team),
            )

        locals_, moves = build((c, g, t), in_refs, out_refs)
        steps = sorted({m.step for m in moves})
        greet = sorted(
            set(steps) | {((-a) % two, (-b) % groups, (-d) % team) for a, b, d in steps}
        )
        barrier = pltpu.get_barrier_semaphore()
        for step in greet:
            pl.semaphore_signal(barrier, inc=1, device_id=device(step), device_id_type=MESH)
        pl.semaphore_wait(barrier, len(greet))

        copies = {}
        arrived = set()
        for k, (src, dst) in enumerate(locals_):
            copies[("local", k)] = pltpu.make_async_copy(src, dst, local_sem.at[k])
        for k, m in enumerate(moves):
            copies[k] = pltpu.make_async_remote_copy(
                src_ref=m.src,
                dst_ref=m.dst,
                send_sem=send_sem.at[k],
                recv_sem=recv_sem.at[k],
                device_id=device(m.step),
                device_id_type=MESH,
            )
        for k, m in enumerate(moves):
            if m.after is None:
                copies[k].start()
        for k in range(len(locals_)):
            copies[("local", k)].start()
        for k, m in enumerate(moves):
            if m.after is not None:
                if m.after not in arrived:
                    arrived.add(m.after)
                    if isinstance(m.after, tuple):
                        copies[m.after].wait()
                    else:
                        copies[m.after].wait_recv()
                copies[k].start()
        for k in range(len(locals_)):
            if ("local", k) not in arrived:
                copies[("local", k)].wait()
        for k in range(len(moves)):
            if k not in arrived:
                copies[k].wait_recv()
        for k in range(len(moves)):
            copies[k].wait_send()

    count = []

    def trace_counts():
        class Probe:
            def __getattr__(self, name):
                return self

            def __getitem__(self, index):
                return self

        locals_, moves = build((0, 0, 0), [Probe() for _ in ins], [Probe() for _ in outs])
        count.extend((len(locals_), len(moves)))

    trace_counts()
    return pl.pallas_call(
        kernel,
        name=name,
        out_shape=tuple(jax.ShapeDtypeStruct(s, d) for s, d in outs),
        in_specs=[pl.BlockSpec(memory_space=pl.ANY)] * len(ins),
        out_specs=tuple(pl.BlockSpec(memory_space=pl.ANY) for _ in outs),
        scratch_shapes=[
            pltpu.SemaphoreType.DMA((max(1, count[1]),)),
            pltpu.SemaphoreType.DMA((max(1, count[1]),)),
            pltpu.SemaphoreType.DMA((max(1, count[0]),)),
        ],
        compiler_params=pltpu.CompilerParams(collective_id=cid, has_side_effects=True),
    )(*ins)


def mask_of(kt, key_place, query_place, query_low):
    return (key_place <= query_place) & (key_place >= query_low)


def key_places(sorted_rows, kt, place_ref):
    if sorted_rows:
        return lax.broadcasted_iota(jnp.int32, (TILE, TILE), 0) + kt * TILE
    return place_ref[pl.ds(pl.multiple_of(kt * TILE, TILE), TILE), :]


def attend_kernel(
    sorted_rows, bounds, meta_ref, place_ref, q_ref, rows_ref, kvt_ref, out_ref, lse_ref
):
    step = pl.program_id(0)
    queries = q_ref[...]
    place, low = meta_ref[0:1, :], meta_ref[1:2, :]

    def body(kt, carry):
        peak, total, acc = carry
        at = pl.ds(pl.multiple_of(kt * TILE, TILE), TILE)
        scores = dot_f32(rows_ref[at, :], queries)
        allowed = mask_of(kt, key_places(sorted_rows, kt, place_ref), place, low)
        scores = jnp.where(allowed, scores, NEG)
        new_peak = jnp.maximum(peak, jnp.max(scores, axis=0, keepdims=True))
        weights = jnp.exp(scores - new_peak)
        fade = jnp.exp(peak - new_peak)
        total = total * fade + jnp.sum(weights, axis=0, keepdims=True)
        acc = acc * fade + dot_f32(kvt_ref[HEAD_DIM:, at], weights.astype(BF))
        return new_peak, total, acc

    start = (
        jnp.full((1, TILE), NEG, F32),
        jnp.zeros((1, TILE), F32),
        jnp.zeros((HEAD_DIM, TILE), F32),
    )
    peak, total, acc = lax.fori_loop(bounds[step, 0], bounds[step, 1], body, start)
    out_ref[...] = acc / total
    lse_ref[...] = peak + jnp.log(total)


def attend_back_kernel(
    sorted_rows,
    tiles,
    bounds,
    meta_ref,
    place_ref,
    q_ref,
    do_ref,
    out_ref,
    lse_ref,
    rows_ref,
    kvt_ref,
    dq_ref,
    dkv_ref,
    acc_ref,
):
    step = pl.program_id(0)

    @pl.when(step == 0)
    def _():
        acc_ref[...] = jnp.zeros_like(acc_ref)

    queries, flows = q_ref[...], do_ref[...]
    place, low = meta_ref[0:1, :], meta_ref[1:2, :]
    log_total = lse_ref[...]
    delta = jnp.sum(flows[HEAD_DIM:, :].astype(F32) * out_ref[...], axis=0, keepdims=True)

    def body(kt, dq):
        at = pl.ds(pl.multiple_of(kt * TILE, TILE), TILE)
        rows = rows_ref[at, :]
        scores = dot_f32(rows, queries)
        allowed = mask_of(kt, key_places(sorted_rows, kt, place_ref), place, low)
        chances = jnp.exp(jnp.where(allowed, scores - log_total, NEG))
        flow = dot_f32(rows, flows)
        score_grad = (chances * (flow - delta)).astype(BF)
        dq = dq + dot_f32(kvt_ref[:HEAD_DIM, at], score_grad)
        acc_ref[:HEAD_DIM, at] += contract_cols(queries[:HEAD_DIM, :], score_grad)
        acc_ref[HEAD_DIM:, at] += contract_cols(flows[HEAD_DIM:, :], chances.astype(BF))
        return dq

    dq = lax.fori_loop(
        bounds[step, 0], bounds[step, 1], body, jnp.zeros((HEAD_DIM, TILE), F32)
    )
    dq_ref[...] = (dq * SCALE).astype(BF)

    @pl.when(step == tiles - 1)
    def _():
        dkv_ref[...] = acc_ref[...].astype(BF)


def attention_specs(length, query_length):
    def whole(shape):
        return pl.BlockSpec(shape, lambda i: (0, 0))

    def tile(rows):
        return pl.BlockSpec((rows, TILE), lambda i: (0, i))

    return whole, tile


def attend(sorted_rows, bounds, meta, place_col, q_pad, kv_rows, kv_t):
    length, query_length = kv_rows.shape[0], q_pad.shape[1]
    whole, tile = attention_specs(length, query_length)
    return pl.pallas_call(
        functools.partial(attend_kernel, sorted_rows),
        name="attend",
        grid=(query_length // TILE,),
        in_specs=[
            pl.BlockSpec(memory_space=pltpu.SMEM),
            tile(8),
            whole(place_col.shape),
            tile(2 * HEAD_DIM),
            whole((length, 2 * HEAD_DIM)),
            whole((2 * HEAD_DIM, length)),
        ],
        out_specs=(tile(HEAD_DIM), tile(1)),
        out_shape=(
            jax.ShapeDtypeStruct((HEAD_DIM, query_length), F32),
            jax.ShapeDtypeStruct((1, query_length), F32),
        ),
        compiler_params=pltpu.CompilerParams(vmem_limit_bytes=40 * 2**20),
    )(bounds, meta, place_col, q_pad, kv_rows, kv_t)


def attend_back(sorted_rows, bounds, meta, place_col, q_pad, do_pad, out, lse, kv_rows, kv_t):
    length, query_length = kv_rows.shape[0], q_pad.shape[1]
    whole, tile = attention_specs(length, query_length)
    return pl.pallas_call(
        functools.partial(attend_back_kernel, sorted_rows, query_length // TILE),
        name="attend_back",
        grid=(query_length // TILE,),
        in_specs=[
            pl.BlockSpec(memory_space=pltpu.SMEM),
            tile(8),
            whole(place_col.shape),
            tile(2 * HEAD_DIM),
            tile(2 * HEAD_DIM),
            tile(HEAD_DIM),
            tile(1),
            whole((length, 2 * HEAD_DIM)),
            whole((2 * HEAD_DIM, length)),
        ],
        out_specs=(tile(HEAD_DIM), whole((2 * HEAD_DIM, length))),
        out_shape=(
            jax.ShapeDtypeStruct((HEAD_DIM, query_length), BF),
            jax.ShapeDtypeStruct((2 * HEAD_DIM, length), BF),
        ),
        scratch_shapes=[pltpu.VMEM((2 * HEAD_DIM, length), F32)],
        compiler_params=pltpu.CompilerParams(vmem_limit_bytes=40 * 2**20),
    )(bounds, meta, place_col, q_pad, do_pad, out, lse, kv_rows, kv_t)


def tall(chunk):
    rows, cols = chunk.shape[-2:]
    factor = 1
    while (rows * factor) % 16:
        factor *= 2
    return chunk.reshape(chunk.shape[:-2] + (rows * factor, cols // factor))


def per_device(
    tokens,
    cotangent,
    block_order,
    doc_lengths,
    routes,
    w_qkv,
    w_out,
    w_up,
    w_down,
    router,
    norm_gains,
    norm_biases,
    expert_up,
    expert_down,
):
    rows, width = tokens.shape[1], tokens.shape[2]
    ctx_count = lax.axis_size("ctx")
    two = lax.axis_size("dp")
    team = math.gcd(4, ctx_count)
    groups = ctx_count // team
    sizes = (two, groups, team)
    team_heads = HEADS // team
    reps = groups // team_heads
    length = rows * ctx_count
    group_rows = rows * team
    experts = ctx_count * expert_up.shape[0]
    capacity = max(2, 2 * rows // experts)
    block_rows = length // block_order.shape[0]
    hidden = w_up.shape[1]
    hidden_dev = w_down.shape[0]
    wr = w_qkv.shape[0]
    qkv_cols = 3 * width // team
    up_cols = hidden // team
    core = lax.axis_index("dp")
    ctx = lax.axis_index("ctx")
    group, member = lax.div(ctx, team), lax.rem(ctx, team)
    team_steps = [(0, 0, k) for k in range(1, team)]
    group_steps = [(0, k, 0) for k in range(1, groups)]
    by_group = [[g * team + t for g in range(groups)] for t in range(team)]
    by_team = [[g * team + t for t in range(team)] for g in range(groups)]
    swap = [(d, (d + 1) % two) for d in range(two)]

    small_flat = jnp.concatenate(
        [router.reshape(-1), norm_gains.reshape(-1), norm_biases.reshape(-1)]
    )
    small_size = -(-small_flat.shape[0] // 2048) * 2048
    small = jnp.pad(small_flat, (0, small_size - small_flat.shape[0])).astype(BF)
    small = small.reshape(-1, 128)

    heads_first = (
        w_qkv.reshape(wr, 3, team, team_heads, HEAD_DIM)
        .transpose(2, 0, 3, 1, 4)
        .reshape(team, wr, qkv_cols)
        .astype(BF)
    )
    up_first = (
        w_up.reshape(wr, two * groups, team, hidden_dev)
        .transpose(2, 0, 1, 3)
        .reshape(team, wr, up_cols)
        .astype(BF)
    )
    heads_first, up_first = tall(heads_first), tall(up_first)
    route_row = jnp.broadcast_to(routes[0, :, 0][None, :], (8, rows))

    def first(coords, ins, outs):
        c, g, t = coords
        moves, local = [], []
        for s in team_steps:
            to = lax.rem(t + s[2], team)
            moves.append(Move(s, ins[0], outs[0].at[t]))
            moves.append(Move(s, ins[1].at[to], outs[1].at[t]))
            moves.append(Move(s, ins[3], outs[3].at[t]))
            moves.append(Move(s, ins[4], outs[4].at[t]))
            moves.append(Move(s, ins[2].at[to], outs[2].at[t]))
        local.append((ins[0], outs[0].at[t]))
        local.append((ins[1].at[t], outs[1].at[t]))
        local.append((ins[2].at[t], outs[2].at[t]))
        local.append((ins[3], outs[3].at[t]))
        local.append((ins[4], outs[4].at[t]))
        return local, moves

    token_rows, qkv_part, up_part, small_part, route_all = exchange(
        "first",
        1,
        sizes,
        (tokens[0], heads_first, up_first, small, route_row),
        [
            ((team, rows, width), BF),
            (heads_first.shape, BF),
            (up_first.shape, BF),
            ((team,) + small.shape, BF),
            ((team, 8, rows), jnp.int32),
        ],
        first,
    )

    def second_build(coords, ins, outs):
        c, g, t = coords
        moves, local = [], []
        for k, s in enumerate(group_steps):
            moves.append(Move(s, ins[0], outs[0].at[c, g]))
            moves.append(Move(s, ins[1], outs[1].at[c, g]))
        for s in team_steps:
            moves.append(Move(s, ins[2], outs[2].at[t]))
        local.append((ins[0], outs[0].at[c, g]))
        local.append((ins[1], outs[1].at[c, g]))
        local.append((ins[2], outs[2].at[t]))
        other = (1, 0, 0)
        for n in range(2):
            moves.append(Move(other, outs[n].at[c, g], outs[n].at[c, g], after=("local", n)))
        for k, s in enumerate(group_steps):
            source = lax.rem(g + groups - s[1], groups)
            for n in range(2):
                moves.append(
                    Move(other, outs[n].at[c, source], outs[n].at[c, source], after=2 * k + n)
                )
        return local, moves

    qkv_all, small_all, cot_rows = exchange(
        "second",
        2,
        sizes,
        (qkv_part, small_part, cotangent[0]),
        [
            ((two, groups) + qkv_part.shape, BF),
            ((two, groups) + small_part.shape, BF),
            ((team, rows, width), BF),
        ],
        second_build,
    )
    qkv_weight = qkv_all.reshape(width, qkv_cols)
    small_rows = small_all.reshape(two * ctx_count, -1)
    router_cols = router.shape[1]
    router_weight = small_rows[:, : wr * router_cols].reshape(width, router_cols)
    vectors = small_rows[:, wr * router_cols : small_flat.shape[0]].reshape(
        two * ctx_count, 4, wr
    )
    vectors = vectors.transpose(1, 0, 2).reshape(4, width).astype(F32)
    gains, shifts = vectors[:2], vectors[2:]

    ff_part = jnp.concatenate(
        [up_part.reshape(team * wr, up_cols), w_down.astype(BF).reshape(team * wr, -1)], axis=1
    )
    ff_half = lax.all_gather(ff_part, "ctx", axis=0, tiled=False, axis_index_groups=by_group)
    out_half = lax.all_gather(w_out.astype(BF), "ctx", axis=0, tiled=True)

    def both(half):
        other = lax.ppermute(half, "dp", swap)
        return jnp.where(core == 0, jnp.stack([half, other]), jnp.stack([other, half]))

    out_weight = both(out_half).reshape(width, width)
    up_weight = both(ff_half[:, :, :up_cols]).reshape(width, up_cols)
    down_weight = both(ff_half[:, :, up_cols:]).reshape(up_cols, width)

    doc_id = jnp.arange(doc_lengths.shape[1], dtype=jnp.int32)
    doc_ends = jnp.sum(
        jnp.where(doc_id[:, None] <= doc_id[None, :], doc_lengths[0][:, None], 0), axis=0
    )
    all_rows = jnp.arange(length, dtype=jnp.int32)
    marks = (all_rows // block_rows)[:, None] == jnp.arange(
        block_order.shape[0], dtype=jnp.int32
    )[None, :]
    anchor = jnp.sum(jnp.where(marks, block_order[None, :], 0), axis=1)
    all_place = anchor * block_rows + all_rows % block_rows

    def low_of(place):
        return jnp.max(
            jnp.where(doc_ends[None, :] <= place[:, None], doc_ends[None, :], 0), axis=1
        )

    sorted_rows = reps == 1
    query_length = length // reps
    tiles = query_length // TILE
    if sorted_rows:
        query_place = all_rows
        order = (all_place[:, None] == all_rows[None, :]).astype(BF)
        lows = low_of(all_rows)
        start = lows[::TILE] // TILE
        bounds = jnp.stack([start, jnp.arange(1, tiles + 1, dtype=jnp.int32)], axis=1)
    else:
        part = lax.rem(group, reps)
        query_place = lax.dynamic_slice(all_place, (part * query_length,), (query_length,))
        lows = low_of(query_place)
        bounds = jnp.broadcast_to(
            jnp.array([[0, length // TILE]], dtype=jnp.int32), (tiles, 2)
        )
    meta = jnp.concatenate(
        [query_place[None], lows[None], jnp.zeros((6, query_length), jnp.int32)], axis=0
    )
    place_col = all_place[:, None] if not sorted_rows else jnp.zeros((8, 128), jnp.int32)

    token_rows = token_rows.reshape(group_rows, width)
    inputs = token_rows.astype(F32)
    normed_low = layer_norm(inputs, gains[0], shifts[0]).astype(BF)
    mixed_t = lax.dot_general(
        qkv_weight, normed_low, (((0,), (1,)), ((), ())), preferred_element_type=F32
    ).astype(BF)
    mixed_t = mixed_t.reshape(team_heads, 3 * HEAD_DIM, group_rows)

    def spread_heads(coords, ins, outs):
        c, g, t = coords
        moves = [
            Move(s, ins[0].at[lax.div(lax.rem(g + s[1], groups), reps)], outs[0].at[g])
            for s in group_steps
        ]
        return [(ins[0].at[lax.div(g, reps)], outs[0].at[g])], moves

    [head_parts] = exchange(
        "heads",
        3,
        sizes,
        (mixed_t,),
        [((groups, 3 * HEAD_DIM, group_rows), BF)],
        spread_heads,
    )
    head_t = head_parts.transpose(1, 0, 2).reshape(3 * HEAD_DIM, length)
    zeros = jnp.zeros((HEAD_DIM, query_length), BF)
    if sorted_rows:
        sorted_t = dot_f32(head_t, order).astype(BF)
        kv_rows = lax.dot_general(
            order, head_t[HEAD_DIM:], (((0,), (1,)), ((), ())), preferred_element_type=F32
        ).astype(BF)
        kv_t = sorted_t[HEAD_DIM:]
        q_t = sorted_t[:HEAD_DIM]
    else:
        kv_t = head_t[HEAD_DIM:]
        kv_rows = kv_t.T
        q_t = lax.dynamic_slice(
            head_t[:HEAD_DIM], (0, part * query_length), (HEAD_DIM, query_length)
        )
    q_pad = jnp.concatenate([q_t * jnp.asarray(SCALE, BF), zeros], axis=0)
    attention_t, log_total = attend(sorted_rows, bounds, meta, place_col, q_pad, kv_rows, kv_t)
    low_t = attention_t.astype(BF)
    if sorted_rows:
        low_t = contract_cols(low_t, order).astype(BF)
    else:
        low_t = lax.dynamic_update_slice(
            jnp.zeros((HEAD_DIM, length), BF), low_t, (0, part * query_length)
        )
    low_t = low_t.reshape(HEAD_DIM, groups, group_rows).transpose(1, 0, 2)

    def gather_heads(coords, ins, outs):
        c, g, t = coords
        moves = [
            Move(s, ins[0].at[lax.rem(g + s[1], groups)], outs[0].at[t, g]) for s in group_steps
        ]
        local = [(ins[0].at[g], outs[0].at[t, g])]
        for s in team_steps:
            moves.append(Move(s, outs[0].at[t, g], outs[0].at[t, g], after=("local", 0)))
        for k, s in enumerate(group_steps):
            source = lax.rem(g + groups - s[1], groups)
            for e in team_steps:
                moves.append(Move(e, outs[0].at[t, source], outs[0].at[t, source], after=k))
        return local, moves

    [attended] = exchange(
        "attended",
        4,
        sizes,
        (low_t,),
        [((team, groups, HEAD_DIM, group_rows), BF)],
        gather_heads,
    )
    if reps > 1:
        chosen = jnp.arange(team_heads) * reps + lax.div(group, groups // reps)
        attended = jnp.take(attended, chosen, axis=1)
    attended_t = attended.reshape(width, group_rows)

    middle = inputs + contract_rows(attended_t, out_weight)
    second_low = layer_norm(middle, gains[1], shifts[1]).astype(BF)
    router_logits = dot_f32(second_low, router_weight)
    route = route_all[:, 0, :]
    earlier = jnp.arange(rows)[None, :] < jnp.arange(rows)[:, None]
    same = (route[:, :, None] == route[:, None, :]) & earlier[None]
    rank = jnp.sum(same.astype(jnp.int32), axis=2)
    route_flat = route.reshape(group_rows)
    route_hot = (route_flat[:, None] == jnp.arange(experts, dtype=jnp.int32)[None, :]).astype(F32)
    gate, mix_dense, mix_expert = router_heads(router_logits, route_hot, experts)
    scaled_gate = mix_expert * gate
    out_grad = cot_rows.reshape(group_rows, width).astype(F32)
    dense_grad = (out_grad * mix_dense[:, None]).astype(BF)
    expert_grad = (out_grad * scaled_gate[:, None]).astype(BF)
    slots = team * capacity
    slot = (jnp.arange(team, dtype=jnp.int32)[:, None] * capacity + rank).reshape(group_rows)
    target = jnp.where(
        route_flat % team == member, (route_flat // team) * slots + slot, groups * slots
    )
    select = (
        jnp.arange(groups * slots, dtype=jnp.int32)[:, None] == target[None, :]
    ).astype(BF)
    send = jnp.concatenate(
        [dot_f32(select, second_low).astype(BF), dot_f32(select, expert_grad).astype(BF)], axis=1
    ).reshape(groups, slots, 2 * width)

    def dispatch(coords, ins, outs):
        c, g, t = coords
        other = (1, 0, 0)
        moves = [
            Move(s, ins[0].at[lax.rem(g + s[1], groups)], outs[0].at[c, g]) for s in group_steps
        ]
        local = [(ins[0].at[g], outs[0].at[c, g])]
        moves.append(Move(other, outs[0].at[c, g], outs[0].at[c, g], after=("local", 0)))
        for k, s in enumerate(group_steps):
            source = lax.rem(g + groups - s[1], groups)
            moves.append(Move(other, outs[0].at[c, source], outs[0].at[c, source], after=k))
        return local, moves

    [arrived] = exchange(
        "dispatch", 5, sizes, (send,), [((two, groups, slots, 2 * width), BF)], dispatch
    )
    arrived = arrived.reshape(two * groups * slots, 2 * width)
    arrived_in, arrived_grad = arrived[:, :width], arrived[:, width:]

    expert_hidden = dot_f32(arrived_in, expert_up[0])
    expert_active = gelu_tanh(expert_hidden).astype(BF)
    partial_out = dot_f32(expert_active, expert_down[0])
    hidden_pull = jax.vjp(gelu_tanh, expert_hidden)[1]
    hidden_grad = hidden_pull(contract_cols(arrived_grad, expert_down[0]))[0].astype(BF)
    input_part = contract_cols(hidden_grad, expert_up[0])
    partial = jnp.concatenate([partial_out, input_part], axis=1).reshape(
        two, groups * slots, 2 * width
    )
    mine = lax.dynamic_index_in_dim(partial, core, 0, keepdims=False)
    theirs = lax.dynamic_index_in_dim(partial, 1 - core, 0, keepdims=False)
    back = (mine + lax.ppermute(theirs, "dp", swap)).astype(BF).reshape(groups, slots, 2 * width)

    def spread(coords, ins, outs):
        c, g, t = coords
        moves = [
            Move(s, ins[0].at[lax.rem(g + s[1], groups)], outs[0].at[g]) for s in group_steps
        ]
        return [(ins[0].at[g], outs[0].at[g])], moves

    [returned] = exchange("returned", 6, sizes, (back,), [(back.shape, BF)], spread)
    returned = returned.reshape(groups * slots, 2 * width)
    expert_down_grad = contract_rows(expert_active, arrived_grad)
    expert_up_grad = contract_rows(arrived_in, hidden_grad)

    upper_residual = dot_f32(second_low, up_weight)
    active_low = gelu_tanh(upper_residual).astype(BF)
    dense_output = dot_f32(active_low, down_weight)
    upper_pull = jax.vjp(gelu_tanh, upper_residual)[1]
    upper_grad = upper_pull(contract_cols(dense_grad, down_weight))[0].astype(BF)
    second_part = contract_cols(upper_grad, up_weight)
    down_term = contract_rows(active_low, dense_grad)
    up_term = contract_rows(second_low, upper_grad)

    picked = contract_rows(select, returned)
    expert_rows, expert_back = picked[:, :width], picked[:, width:]
    layer_part = mix_dense[:, None] * dense_output + scaled_gate[:, None] * expert_rows
    sums_part = jnp.stack(
        [jnp.sum(out_grad * dense_output, axis=1), jnp.sum(out_grad * expert_rows, axis=1)]
    )
    sums_part = jnp.pad(
        sums_part.reshape(2, team, rows).transpose(1, 0, 2), ((0, 0), (0, 6), (0, 0))
    )
    both_part = (
        jnp.concatenate([layer_part, second_part + expert_back], axis=1)
        .astype(BF)
        .reshape(team, rows, 2 * width)
    )

    def to_owner(coords, ins, outs):
        c, g, t = coords
        moves, local = [], []
        for n in range(len(ins)):
            for s in team_steps:
                moves.append(Move(s, ins[n].at[lax.rem(t + s[2], team)], outs[n].at[t]))
            local.append((ins[n].at[t], outs[n].at[t]))
        return local, moves

    both_own, sums_own = exchange(
        "owner",
        7,
        sizes,
        (both_part, sums_part),
        [(both_part.shape, BF), (sums_part.shape, F32)],
        to_owner,
    )
    both_own = jnp.sum(both_own.astype(F32), axis=0)
    sums_own = jnp.sum(sums_own, axis=0)

    def own(array):
        return lax.dynamic_slice_in_dim(array, member * rows, rows, axis=0)

    middle_own, logits_own, hot_own, second_own = (
        own(middle),
        own(router_logits),
        own(route_hot),
        own(second_low),
    )
    out_grad_own = cotangent[0].astype(F32)
    layer_out = middle_own + both_own[:, :width]
    (gate_own, mix_dense_own, mix_expert_own), router_pull = jax.vjp(
        lambda values: router_heads(values, hot_own, experts), logits_own
    )
    logit_grad = router_pull(
        (sums_own[1] * mix_expert_own, sums_own[0], sums_own[1] * gate_own)
    )[0].astype(BF)
    router_term = contract_rows(second_own, logit_grad)
    second_grad = both_own[:, width:] + contract_cols(logit_grad, router_weight)
    middle_part, gain_second, bias_second = jax.vjp(layer_norm, middle_own, gains[1], shifts[1])[1](
        second_grad
    )
    middle_grad = out_grad_own + middle_part
    branch_grad = middle_grad.astype(BF)
    attended_own = lax.dynamic_slice_in_dim(attended_t, member * rows, rows, axis=1)
    out_term = dot_f32(attended_own, branch_grad)
    flow_t = contract_cols(out_weight, branch_grad).astype(BF)
    flow_t = flow_t.reshape(team, team_heads, HEAD_DIM, rows)

    def spread_flow(coords, ins, outs):
        c, g, t = coords
        moves = []
        for dg in range(groups):
            for dt in range(team):
                if dg or dt:
                    to_g, to_t = lax.rem(g + dg, groups), lax.rem(t + dt, team)
                    moves.append(
                        Move((0, dg, dt), ins[0].at[to_t, lax.div(to_g, reps)], outs[0].at[g, t])
                    )
        return [(ins[0].at[t, lax.div(g, reps)], outs[0].at[g, t])], moves

    [flow_parts] = exchange(
        "flow", 8, sizes, (flow_t,), [((groups, team, HEAD_DIM, rows), BF)], spread_flow
    )
    flow_all = flow_parts.transpose(2, 0, 1, 3).reshape(HEAD_DIM, length)
    if sorted_rows:
        flow_all = dot_f32(flow_all, order).astype(BF)
    else:
        flow_all = lax.dynamic_slice(
            flow_all, (0, part * query_length), (HEAD_DIM, query_length)
        )
    do_pad = jnp.concatenate([zeros, flow_all], axis=0)
    query_grad, pair_grad = attend_back(
        sorted_rows,
        bounds,
        meta,
        place_col,
        q_pad,
        do_pad,
        attention_t,
        log_total,
        kv_rows,
        kv_t,
    )
    if not sorted_rows:
        query_grad = lax.dynamic_update_slice(
            jnp.zeros((HEAD_DIM, length), BF), query_grad, (0, part * query_length)
        )
    grad_t = jnp.concatenate([query_grad, pair_grad], axis=0)
    if sorted_rows:
        grad_t = contract_cols(grad_t, order).astype(BF)
    grad_t = grad_t.reshape(3 * HEAD_DIM, groups, group_rows).transpose(1, 0, 2)
    [grad_parts] = exchange("mixed", 9, sizes, (grad_t,), [(grad_t.shape, BF)], spread)
    if reps > 1:
        grad_parts = jnp.sum(
            grad_parts.reshape(team_heads, reps, 3 * HEAD_DIM, group_rows).astype(F32), axis=1
        ).astype(BF)
    mixed_grad_t = grad_parts.reshape(qkv_cols, group_rows)
    normed_part = (
        lax.dot_general(
            mixed_grad_t, qkv_weight, (((0,), (1,)), ((), ())), preferred_element_type=F32
        )
        .astype(BF)
        .reshape(team, rows, width)
    )
    qkv_term = lax.dot_general(
        normed_low, mixed_grad_t, (((0,), (1,)), ((), ())), preferred_element_type=F32
    )
    [normed_own] = exchange(
        "normed", 10, sizes, (normed_part,), [(normed_part.shape, BF)], to_owner
    )
    normed_grad = jnp.sum(normed_own.astype(F32), axis=0)
    input_part_grad, gain_first, bias_first = jax.vjp(
        layer_norm, tokens[0].astype(F32), gains[0], shifts[0]
    )[1](normed_grad)
    input_grad = middle_grad + input_part_grad

    def core_half(term):
        halves = term.reshape((two, term.shape[0] // two) + term.shape[1:])
        keep = lax.dynamic_index_in_dim(halves, core, 0, keepdims=False)
        give = lax.dynamic_index_in_dim(halves, 1 - core, 0, keepdims=False)
        return keep + lax.ppermute(give.astype(BF), "dp", swap).astype(F32)

    def over_groups(term):
        return lax.psum_scatter(
            core_half(term).astype(BF),
            "ctx",
            scatter_dimension=0,
            tiled=True,
            axis_index_groups=by_group,
        )

    down_sum = over_groups(down_term).astype(F32)
    up_sum = over_groups(up_term).reshape(team, wr, up_cols)
    out_sum = lax.psum_scatter(
        core_half(out_term).astype(BF), "ctx", scatter_dimension=0, tiled=True
    ).astype(F32)
    qkv_sum = over_groups(qkv_term).reshape(team, wr, qkv_cols)
    up_own, qkv_own = exchange(
        "owners",
        11,
        sizes,
        (tall(up_sum), tall(qkv_sum)),
        [(tall(up_sum).shape, BF), (tall(qkv_sum).shape, BF)],
        to_owner,
    )
    up_own = (
        up_own.reshape(team, wr, two * groups, hidden_dev)
        .transpose(1, 2, 0, 3)
        .reshape(wr, hidden)
        .astype(F32)
    )
    qkv_own = (
        qkv_own.reshape(team, wr, team_heads, 3, HEAD_DIM)
        .transpose(1, 3, 0, 2, 4)
        .reshape(wr, 3 * width)
        .astype(F32)
    )
    small_term = jnp.concatenate(
        [
            router_term,
            gain_first[:, None],
            gain_second[:, None],
            bias_first[:, None],
            bias_second[:, None],
        ],
        axis=1,
    )
    small_sum = lax.psum_scatter(small_term, ("dp", "ctx"), scatter_dimension=0, tiled=True)
    vector_sums = small_sum[:, router_cols:].T
    return (
        layer_out[None].astype(BF),
        input_grad[None].astype(BF),
        qkv_own,
        out_sum,
        up_own,
        down_sum,
        small_sum[:, :router_cols],
        vector_sums[:2],
        vector_sums[2:],
        expert_up_grad[None],
        expert_down_grad[None],
    )


def solution(mesh):
    in_specs = (
        P("dp", "ctx", None),
        P("dp", "ctx", None),
        P(),
        P("dp", None),
        P("dp", "ctx", None),
        P(("dp", "ctx"), None),
        P(("dp", "ctx"), None),
        P(("dp", "ctx"), None),
        P(("dp", "ctx"), None),
        P(("dp", "ctx"), None),
        P(None, ("dp", "ctx")),
        P(None, ("dp", "ctx")),
        P("ctx", None, "dp"),
        P("ctx", "dp", None),
    )
    out_specs = (
        P("dp", "ctx", None),
        P("dp", "ctx", None),
        P(("dp", "ctx"), None),
        P(("dp", "ctx"), None),
        P(("dp", "ctx"), None),
        P(("dp", "ctx"), None),
        P(("dp", "ctx"), None),
        P(None, ("dp", "ctx")),
        P(None, ("dp", "ctx")),
        P("ctx", None, "dp"),
        P("ctx", "dp", None),
    )
    return jax.shard_map(
        per_device, mesh=mesh, in_specs=in_specs, out_specs=out_specs, check_vma=False
    )
```

time: 2540 us -> 700 us (0.28)
  waiting for transfers between devices: 1880 us -> 249 us
  blocking collectives: 325 us -> 0 us
  Pallas kernels: 0 us -> 241 us
  matrix products: 161 us -> 82.7 us
  local copies, waits for them, and re-layouts: 99.9 us -> 46.2 us
    reduce_scatter x5 -> x4, waiting for transfers between devices: 1370 us -> 141 us  [the longest x3 73.8 us: over_groups(): lax.psum_scatter(core_half(term).astype(BF), 'ctx', scatter_dimension=0,...]
    unnamed x16 -> x8, waiting for transfers between devices: 364 us -> 100 us
    all_gather x3 -> x0, blocking collectives: 252 us -> none  [the longest x1 119 us: per_device(): lax.all_gather(masters[4], ('dp', 'ctx'), axis=0, tiled=True)]
    pallas_call x0 -> x13, Pallas kernels: none -> 241 us  [the longest x11 220 us: exchange(): pl.pallas_call(kernel, name=name, out_shape=tuple((jax.ShapeDtypeStruct(s...]
    all_gather x5 -> x2, waiting for transfers between devices: 108 us -> 0.01 us  [the longest x1 0.01 us: per_device(): out_half = lax.all_gather(w_out.astype(BF), 'ctx', axis=0, tiled=True)]
    all_to_all x2 -> x0, blocking collectives: 73.1 us -> none  [the longest x1 42.2 us: per_device(): lax.all_to_all(jnp.concatenate([send, send], axis=0), ('dp', 'ctx'), spli...]
    dot_general x23 -> x14, matrix products: 89.3 us -> 36.4 us  [the longest x10 24.3 us: dot_f32(): return jnp.dot(left, right, preferred_element_type=F32)]
    all_to_all x2 -> x0, waiting for transfers between devices: 35.4 us -> none  [the longest x1 35.4 us: per_device(): lax.all_to_all(input_part, ('dp', 'ctx'), split_axis=0, concat_axis=0, ti...]
  transfers between devices with their start and end apart: 15 -> 15, of which waited for: 10 -> 8; matrix products, arithmetic and copies ran while one was open for 7% -> 25% of each run, Pallas kernels for 0% -> 35%
where the time goes in v1:
time: 700 us; the launch traced here: 689 us
  waiting for transfers between devices  249 us (36%)
  Pallas kernels  241 us (34%)
  matrix products  82.7 us (12%)
  other arithmetic  51.5 us (7%)
  local copies, waits for them, and re-layouts  46.2 us (7%)
  between operations  15.9 us (2%)
    pallas_call x11, Pallas kernels, exchange(): pl.pallas_call(kernel, name=name, out_shape=tuple((jax.ShapeDtypeStruct(s...  220 us
    unnamed x8, waiting for transfers between devices  100 us
    reduce_scatter x3, waiting for transfers between devices, over_groups(): lax.psum_scatter(core_half(term).astype(BF), 'ctx', scatter_dimension=0,...  73.8 us
    reduce_scatter x1, waiting for transfers between devices, per_device(): lax.psum_scatter(core_half(out_term).astype(BF), 'ctx', scatter_dimension...  67.2 us
    dot_general x10, matrix products, dot_f32(): return jnp.dot(left, right, preferred_element_type=F32)  24.3 us
    dot_general x8, matrix products, contract_cols(): lax.dot_general(left, right, (((1,), (1,)), ((), ())), preferred_element_...  23.2 us
    dot_general x7, matrix products, contract_rows(): lax.dot_general(left, right, (((0,), (0,)), ((), ())), preferred_element_...  23.1 us
  transfers between devices with their start and end apart: 15, of which 8 were waited for; matrix products, arithmetic and copies ran while one was open for 25% of the time, Pallas kernels for 35%

profile of v1, /device:TPU:0, one launch (start us, length us, event | category | flops | bytes accessed | tf_op | source)
XLA Modules:
  0.0 688.6 jit_solution(9812934623044809814)
XLA Ops:
  14.3 22.5 %first.1 = (bf16[4,128,1024]{2,1,0:T(8,128)(2,1)}, bf16[4,32,768]{2,1,0:T(8,128)(2,1)}, bf16[4,32,1024]{2,1,0:T(8,128)(2,1)}, bf16[4,16,128]{2,1,0:T(8,128)(2,1)}, s32[4,8,128]{2,1,0:T(8,128)}) custom-call(bf16[128,1024]{1,0:T(8,128)(2,1)} %bitcast.249, bf16[4,32,768]{2,1,0:T(8,128)(2,1)} %convert_element_type.253.refs_1_, ...), custom_call_target="tpu_custom_call" | custom-call | tf_op jit(solution)/shard_map/first/pallas_call | solution.py:134
  40.6 23.3 %second.1 = (bf16[2,4,4,32,768]{4,3,2,1,0:T(8,128)(2,1)}, bf16[2,4,4,16,128]{4,3,2,1,0:T(8,128)(2,1)}, bf16[4,128,1024]{2,1,0:T(8,128)(2,1)}) custom-call(bf16[4,32,768]{2,1,0:T(8,128)(2,1)} %get-tuple-element.28.refs_0_, bf16[4,16,128]{2,1,0:T(8,128)(2,1)} %get-tuple-element.29.refs_1_, bf16[128,1024]{1,0:T(8,128)(2,1)} %bitcast.266), custom_call_target="tpu_custom_call" | custom-call | tf_op jit(solution)/shard_map/second/pallas_call | solution.py:134
  69.0 20.9 %heads.1 = bf16[4,192,512]{2,1,0:T(8,128)(2,1)} custom-call(bf16[4,192,512]{2,1,0:T(8,128)(2,1)} %bitcast.290), custom_call_target="tpu_custom_call" | custom-call | tf_op jit(solution)/shard_map/heads/pallas_call | solution.py:134
  95.5 4.9 fusion.29.rows_ref
  101.0 9.8 %attend.1 = (f32[64,2048]{1,0:T(8,128)S(1)}, f32[1,2048]{1,0:T(1,128)S(1)}) custom-call(s32[8,2]{1,0:T(8,128)S(1)} %copy.76.bounds, s32[8,2048]{1,0:T(8,128)S(1)} %add_add_fusion.3.meta_ref, s32[8,128]{1,0:T(8,128)S(1)} %broadcast_in_dim.84.place_ref, bf16[128,2048]{1,0:T(8,128)(2,1)S(1)} %concatenate.40.q_ref, bf16[2048,128]{1,0:T(8,128)(2,1)S(1)} %fusion.29.rows_ref, ...), custom_call_target="tpu_custom_call" | custom-call | tf_op jit(solution)/shard_map/attend/pallas_call | solution.py:252
  118.2 24.9 %attended.1 = bf16[4,4,64,512]{3,2,1,0:T(8,128)(2,1)} custom-call(bf16[4,64,512]{2,1,0:T(8,128)(2,1)} %bitcast.280), custom_call_target="tpu_custom_call" | custom-call | tf_op jit(solution)/shard_map/attended/pallas_call | solution.py:134
  157.9 24.2 %dispatch.1 = bf16[2,4,64,2048]{3,2,1,0:T(8,128)(2,1)} custom-call(bf16[4,64,2048]{2,1,0:T(8,128)(2,1)} %bitcast.254), custom_call_target="tpu_custom_call" | custom-call | tf_op jit(solution)/shard_map/dispatch/pallas_call | solution.py:134
  182.1 5.0 fusion.23
  187.1 5.2 fusion.16
  233.2 25.2 %returned.1 = bf16[4,64,2048]{2,1,0:T(8,128)(2,1)} custom-call(bf16[4,64,2048]{2,1,0:T(8,128)(2,1)} %bitcast.260), custom_call_target="tpu_custom_call" | custom-call | tf_op jit(solution)/shard_map/returned/pallas_call | solution.py:134
  267.2 26.7 %owner.1 = (bf16[4,128,2048]{2,1,0:T(8,128)(2,1)}, f32[4,8,128]{2,1,0:T(8,128)}) custom-call(bf16[4,128,2048]{2,1,0:T(8,128)(2,1)} %pad_maximum_fusion.1.refs_0_, f32[4,8,128]{2,1,0:T(8,128)} %pad.24.refs_1_), custom_call_target="tpu_custom_call" | custom-call | tf_op jit(solution)/shard_map/owner/pallas_call | solution.py:134
  306.7 15.2 %flow.1 = bf16[4,4,64,128]{3,2,1,0:T(8,128)(2,1)} custom-call(bf16[4,4,64,128]{3,2,1,0:T(8,128)(2,1)} %bitcast.281), custom_call_target="tpu_custom_call" | custom-call | tf_op jit(solution)/shard_map/flow/pallas_call | solution.py:134
  325.6 4.4 fusion.31
  330.1 11.4 %attend_back.1 = (bf16[64,2048]{1,0:T(8,128)(2,1)S(1)}, bf16[128,2048]{1,0:T(8,128)(2,1)S(1)}) custom-call(s32[8,2]{1,0:T(8,128)S(1)} %copy.76.bounds, s32[8,2048]{1,0:T(8,128)S(1)} %add_add_fusion.3.meta_ref, s32[8,128]{1,0:T(8,128)S(1)} %broadcast_in_dim.84.place_ref, bf16[128,2048]{1,0:T(8,128)(2,1)S(1)} %concatenate.40.q_ref, ...), custom_call_target="tpu_custom_call" | custom-call | tf_op jit(solution)/shard_map/attend_back/pallas_call | solution.py:276
  346.4 16.8 %mixed.1 = bf16[4,192,512]{2,1,0:T(8,128)(2,1)} custom-call(bf16[4,192,512]{2,1,0:T(8,128)(2,1)} %bitcast.265), custom_call_target="tpu_custom_call" | custom-call | tf_op jit(solution)/shard_map/mixed/pallas_call | solution.py:134
  366.4 13.2 %normed.1 = bf16[4,128,1024]{2,1,0:T(8,128)(2,1)} custom-call(bf16[4,128,1024]{2,1,0:T(8,128)(2,1)} %bitcast.283), custom_call_target="tpu_custom_call" | custom-call | tf_op jit(solution)/shard_map/normed/pallas_call | solution.py:134
  406.6 7.9 %convolution_bitcast_fusion.1 = f32[1,1024,2048]{2,1,0:T(8,128)} fusion(bf16[512,2048]{1,0:T(8,128)(2,1)} %copy-done.70, bf16[512,2048]{1,0:T(8,128)(2,1)} %bitcast.269), kind=kOutput, calls=%fused_computation.14 | convolution fusion | flops 2147483648 | bytes 11534336 | tf_op jit(solution)/shard_map/dot_general | solution.py:45
  414.5 6.3 convolution_bitcast_fusion
  421.7 100.3 %reduce-scatter.16.cloned.1.call-done = f32[32,22]{1,0:T(8,128)} async-done(((f32[1024,22]{1,0:T(8,128)}), f32[32,22]{1,0:T(8,128)}) %reduce-scatter.16.cloned.1.call-update) | async-done | bytes 2832
  524.9 23.4 %reduce-scatter.14.cloned.1.call-done = bf16[128,1024]{1,0:T(8,128)(2,1)} async-done(((bf16[512,1024]{1,0:T(8,128)(2,1)}), bf16[128,1024]{1,0:T(8,128)(2,1)}) %reduce-scatter.14.cloned.1.call-update) | async-done | bytes 262160 | tf_op jit(solution)/shard_map/reduce_scatter | solution.py:796
  550.0 26.2 %reduce-scatter.8.cloned.1.call-done = bf16[128,1024]{1,0:T(8,128)(2,1)} async-done(((bf16[512,1024]{1,0:T(8,128)(2,1)}), bf16[128,1024]{1,0:T(8,128)(2,1)}) %reduce-scatter.8.cloned.1.call-update) | async-done | bytes 262160 | tf_op jit(solution)/shard_map/reduce_scatter | solution.py:796
  576.2 24.3 %reduce-scatter.10.cloned.1.call-done = bf16[128,768]{1,0:T(8,128)(2,1)} async-done(((bf16[512,768]{1,0:T(8,128)(2,1)}), bf16[128,768]{1,0:T(8,128)(2,1)}) %reduce-scatter.10.cloned.1.call-update) | async-done | bytes 196624 | tf_op jit(solution)/shard_map/reduce_scatter | solution.py:796
  600.5 7.4 %owners.1 = (bf16[4,32,1024]{2,1,0:T(8,128)(2,1)}, bf16[4,32,768]{2,1,0:T(8,128)(2,1)}) custom-call(bf16[4,32,1024]{2,1,0:T(8,128)(2,1)} %bitcast.293, bf16[4,32,768]{2,1,0:T(8,128)(2,1)} %bitcast.299), custom_call_target="tpu_custom_call" | custom-call | tf_op jit(solution)/shard_map/owners/pallas_call | solution.py:134
  612.6 67.2 %reduce-scatter.12.cloned.1.call-done = bf16[32,1024]{1,0:T(8,128)(2,1)} async-done(((bf16[512,1024]{1,0:T(8,128)(2,1)}), bf16[32,1024]{1,0:T(8,128)(2,1)}) %reduce-scatter.12.cloned.1.call-update) | async-done | bytes 65552 | tf_op jit(solution)/shard_map/reduce_scatter | solution.py:806
  (355 shorter events, 156.3 us)
Async XLA Ops:
  7.2 108.0 %all-gather.4.cloned.1.call-start = ((), (), s32[]{:S(2)}) async-start(), calls=%async_computation.5 | async-start | bytes 1114112 | tf_op jit(solution)/shard_map/all_gather | solution.py:454
  8.8 194.8 %all-gather.6.cloned.1.call-start = ((), (), s32[]{:S(2)}) async-start(), calls=%async_computation.10 | async-start | bytes 2621440 | tf_op jit(solution)/shard_map/all_gather | solution.py:453
  38.8 483.2 %reduce-scatter.16.cloned.1.call-start = ((), (), s32[]{:S(2)}) async-start(), calls=%async_computation.11 | async-start | bytes 540672
  69.0 22.1 %copy-start.62 = (s32[32]{0:T(128)S(1)}, s32[32]{0:T(128)}, u32[]{:S(2)}) copy-start(s32[32]{0:T(128)} %param.16) | copy-start | bytes 388
  91.3 19.5 %copy-start.48 = (s32[2048]{0:T(1024)}, s32[2048]{0:T(1024)S(1)}, u32[]{:S(2)}) copy-start(s32[2048]{0:T(1024)S(1)} %fusion.118) | copy-start | bytes 24580
  115.2 31.8 %copy-start.12 = (bf16[1,128,1024]{2,1,0:T(8,128)(2,1)S(1)}, bf16[1,128,1024]{2,1,0:T(8,128)(2,1)}, u32[]{:S(2)}) copy-start(bf16[1,128,1024]{2,1,0:T(8,128)(2,1)} %param.14) | copy-start | bytes 786436
  115.2 33.8 %collective-permute-start = (bf16[512,1024]{1,0:T(8,128)(2,1)}, bf16[512,1024]{1,0:T(8,128)(2,1)}, u32[]{:S(2)}, u32[]{:S(2)}) collective-permute-start(bf16[512,1024]{1,0:T(8,128)(2,1)} %all-gather.4.cloned.1.call-done), channel_id=1, source_target_pairs={{0,16},{16,0},{1,17},{17,1},{2,18},{18,2},{3,19},{19,3},{4,20},{20... | collective-permute-start | bytes 3145736 | tf_op jit(solution)/shard_map/ppermute | solution.py:457
  200.7 29.7 %collective-permute-start.3 = (f32[256,2048]{1,0:T(8,128)}, f32[256,2048]{1,0:T(8,128)}, u32[]{:S(2)}, u32[]{:S(2)}) collective-permute-start(f32[256,2048]{1,0:T(8,128)} %dynamic-slice_bitcast_fusion), channel_id=1, source_target_pairs={{0,16},{16,0},{1,17},{17,1},{2,18},{18,2},{3,19},{19,3},{4,20},{20... | collective-permute-start | bytes 6291464 | tf_op jit(solution)/shard_map/ppermute | solution.py:634
  207.3 3.9 collective-permute-start.1
  210.8 13.4 %collective-permute-start.2 = (bf16[4,128,1024]{2,1,0:T(8,128)(2,1)}, bf16[4,128,1024]{2,1,0:T(8,128)(2,1)}, u32[]{:S(2)}, u32[]{:S(2)}) collective-permute-start(bf16[4,128,1024]{2,1,0:T(8,128)(2,1)} %get-tuple-element.68), channel_id=1, source_target_pairs={{0,16},{16,0},{1,17},{17,1},{2,18},{18,2},{3,19},{19,3},{4,20},{20... | collective-permute-start | bytes 3145736 | tf_op jit(solution)/shard_map/ppermute | solution.py:457
  224.1 159.2 %collective-permute-start.7 = (bf16[512,1024]{1,0:T(8,128)(2,1)}, bf16[512,1024]{1,0:T(8,128)(2,1)}, u32[]{:S(2)}, u32[]{:S(2)}) collective-permute-start(bf16[512,1024]{1,0:T(8,128)(2,1)} %fusion.70), channel_id=1, source_target_pairs={{0,16},{16,0},{1,17},{17,1},{2,18},{18,2},{3,19},{19,3},{4,20},{20... | collective-permute-start | bytes 3145736 | tf_op jit(solution)/shard_map/ppermute | solution.py:793
  267.2 29.6 %copy-start.51 = (f32[128]{0:T(128)S(1)}, f32[128]{0:T(128)}, u32[]{:S(2)}) copy-start(f32[128]{0:T(128)} %dynamic-slice_reduce_fusion.1) | copy-start | bytes 1540
  305.3 20.3 %copy-start.49 = (s32[2048]{0:T(1024)S(1)}, s32[2048]{0:T(1024)}, u32[]{:S(2)}) copy-start(s32[2048]{0:T(1024)} %copy-done.48) | copy-start | bytes 24580
  345.5 17.8 %copy-start.66 = (bf16[2,4,4,32,768]{4,3,2,1,0:T(8,128)(2,1)S(1)}, bf16[2,4,4,32,768]{4,3,2,1,0:T(8,128)(2,1)}, u32[]{:S(2)}) copy-start(bf16[2,4,4,32,768]{4,3,2,1,0:T(8,128)(2,1)} %get-tuple-element.30) | copy-start | bytes 4718596
  366.4 13.3 %copy-start.6 = (bf16[512,1024]{1,0:T(8,128)(2,1)S(1)}, bf16[512,1024]{1,0:T(8,128)(2,1)}, u32[]{:S(2)}) copy-start(bf16[512,1024]{1,0:T(8,128)(2,1)} %copy-done.4) | copy-start | bytes 3145732
  366.4 13.3 %copy-start.43 = (f32[128,2]{0,1:T(2,128)S(1)}, f32[128,2]{0,1:T(2,128)}, u32[]{:S(2)}) copy-start(f32[128,2]{0,1:T(2,128)} %copy-done.42) | copy-start | bytes 3076
  366.4 15.1 %copy-start.55 = (f32[128]{0:T(128)S(1)}, f32[128]{0:T(128)}, u32[]{:S(2)}) copy-start(f32[128]{0:T(128)} %broadcast_multiply_fusion.2) | copy-start | bytes 1540
  383.2 165.0 %reduce-scatter.14.cloned.1.call-start = ((), (), s32[]{:S(2)}) async-start(), calls=%async_computation.9 | async-start | bytes 1310720 | tf_op jit(solution)/shard_map/reduce_scatter | solution.py:796
  386.6 189.6 %reduce-scatter.8.cloned.1.call-start = ((), (), s32[]{:S(2)}) async-start(), calls=%async_computation.6 | async-start | bytes 1310720 | tf_op jit(solution)/shard_map/reduce_scatter | solution.py:796
  389.3 2.7 collective-permute-start.4
  393.5 207.0 %reduce-scatter.10.cloned.1.call-start = ((), (), s32[]{:S(2)}) async-start(), calls=%async_computation.7 | async-start | bytes 983040 | tf_op jit(solution)/shard_map/reduce_scatter | solution.py:796
  396.8 2.4 collective-permute-start.5
  400.3 279.5 %reduce-scatter.12.cloned.1.call-start = ((), (), s32[]{:S(2)}) async-start(), calls=%async_computation.8 | async-start | bytes 1114112 | tf_op jit(solution)/shard_map/reduce_scatter | solution.py:806
  402.4 2.7 collective-permute-start.6
  (66 other events, 222.3 us)
Sparse Core Ops, SparseCore 0:
  11.4 66.0 all-gather.3
  79.6 57.1 all-gather.5
  383.3 138.6 reduce-scatter.15
  524.3 23.9 reduce-scatter.13
  550.4 25.7 reduce-scatter.7
  578.5 21.9 reduce-scatter.9
  602.8 76.8 reduce-scatter.11
